TPU v7x, 256 devices: a whole 4x4x8 slice. The times are simulated.
256 devices in a mesh: lang: 8 (over x, core), dp: 32 (over z, y).
Axes of the slice: x: 4, y: 4, z: 8, core: 2. Of those that a mesh axis runs over, the one named last changes fastest.
Arguments:
- src_emb: bfloat16 [32768, 768], P(('lang', 'dp')), may hold values from -6 to 6
- tgt_emb: bfloat16 [8, 4096, 768], P(None, ('lang', 'dp')), may hold values from -6 to 6
- slot_group: int32 [8], replicated, may hold values from 0 to 7, each once
- counts: int32 [8], replicated, may hold values from 1024 to 4096, as said below
- align: int32 [8, 4096], P('lang'), may hold values from 0 to 4095, each once within a row
- pair_weight: float32 [8], replicated, may hold values from 4 to 40
Outputs:
- grad_src: bfloat16 [32768, 768], P(('lang', 'dp'))
- grad_tgt: bfloat16 [8, 4096, 768], P(None, ('lang', 'dp'))
- pair_loss: float32 [8], P('lang')
Inputs may be any that keep to these rules, and one draw needn't show every extreme that they name: `counts`: at least one pair has all 4096 sentences live. `align`: each row is a permutation.
All inputs are finite; a program needn't handle non-finite values.
Results may differ from a plain program's by a relative error of at most 0.0057.
Values may be sent and summed in bfloat16 or wider, within the bound.
A program may use at most 64 MiB of HBM per device.

v0:
```python
import math
import jax
import jax.numpy as jnp
from jax import lax
from jax.sharding import PartitionSpec as P

MARGIN = 0.3
LOW_FILL = -1e30


def combined_all(value, axis, combine):
    everything = jax.tree.map(lambda part: lax.all_gather(part, axis), value)
    initial = jax.tree.map(lambda part: part[0], everything)

    def lap(k, so_far):
        return combine(so_far, jax.tree.map(lambda part: part[k], everything))

    return lax.fori_loop(1, lax.axis_size(axis), lap, initial)


def target_index(offset, col_count, row_count, per_slot, data_size):
    position = offset + jnp.arange(col_count, dtype=jnp.int32)
    source = position // row_count
    within = position % row_count
    return (within // per_slot * data_size + source) * per_slot + within % per_slot


def tile_scores(
    src_rows, tile_rows, offset, my_align, col_live_global, per_slot, data_size, inv_root
):
    row_count = src_rows.shape[0]
    tgt_index = target_index(offset, tile_rows.shape[0], row_count, per_slot, data_size)
    raw_dot = lax.dot_general(
        src_rows, tile_rows, (((1,), (1,)), ((), ())), preferred_element_type=jnp.float32
    )
    is_pos = tgt_index[None, :] == my_align[:, None]
    scores_f = raw_dot * inv_root - MARGIN * is_pos.astype(jnp.float32)
    col_ok = col_live_global[tgt_index] > 0.5
    return (scores_f, is_pos, col_ok)


def row_update(old_max, scores_f, col_ok):
    masked = jnp.where(col_ok[None, :], scores_f, LOW_FILL)
    new_max = jnp.maximum(old_max, jnp.max(masked, axis=1))
    fresh = jnp.sum(jnp.where(col_ok[None, :], jnp.exp(scores_f - new_max[:, None]), 0.0), axis=1)
    return (new_max, fresh)


def column_stats(scores_f, row_live):
    col_max = jnp.max(jnp.where(row_live[:, None], scores_f, LOW_FILL), axis=0)
    col_sum = jnp.sum(
        jnp.where(row_live[:, None], jnp.exp(scores_f - col_max[None, :]), 0.0), axis=0
    )
    return (col_max, col_sum)


def grad_block(scores_f, is_pos, col_ok, row_lse, col_lse_all, row_live, weight):
    both_live = row_live[:, None] & col_ok[None, :]
    by_row = jnp.where(both_live, jnp.exp(scores_f - row_lse[:, None]), 0.0)
    by_col = jnp.where(both_live, jnp.exp(scores_f - col_lse_all[None, :]), 0.0)
    pos_hit = (is_pos & row_live[:, None]).astype(jnp.float32)
    return (weight * (by_row + by_col - 2.0 * pos_hit)).astype(jnp.bfloat16)


def merge_columns(first_part, second_part):
    top_val = jnp.maximum(first_part[0], second_part[0])
    summed = first_part[1] * jnp.exp(first_part[0] - top_val) + second_part[1] * jnp.exp(
        second_part[0] - top_val
    )
    return (top_val, summed)


def per_device(src_emb, tgt_emb, slot_group, counts, align, pair_weight):
    lang_size = lax.axis_size("lang")
    data_size = lax.axis_size("dp")
    row_count, emb_width = src_emb.shape
    per_slot = tgt_emb.shape[1]
    pair_rows = row_count * data_size
    inv_root = 1.0 / math.sqrt(emb_width)
    group_index = lax.axis_index("lang")
    shard_index = lax.axis_index("dp")
    slot_ids = jnp.arange(lang_size, dtype=jnp.int32)
    slot_of_group = jnp.zeros((lang_size,), jnp.int32).at[slot_group].set(slot_ids)
    ordered = tgt_emb[slot_of_group]
    arrived = lax.all_to_all(ordered, "lang", split_axis=0, concat_axis=1, tiled=True)
    partner = arrived[0]
    live_count = counts[group_index]
    weight = pair_weight[group_index]
    pair_align = align[0]
    all_rows = jnp.arange(pair_rows, dtype=jnp.int32)
    col_live_global = (
        jnp.zeros((pair_rows,), jnp.float32)
        .at[pair_align]
        .set((all_rows < live_count).astype(jnp.float32))
    )
    my_rows = shard_index * row_count + jnp.arange(row_count, dtype=jnp.int32)
    row_live = my_rows < live_count
    my_align = lax.dynamic_slice_in_dim(pair_align, shard_index * row_count, row_count)
    gathered_index = target_index(0, pair_rows, row_count, per_slot, data_size)
    col_live_gathered = col_live_global[gathered_index]
    start_max = jnp.full((row_count,), LOW_FILL, jnp.float32)
    all_targets = lax.all_gather(partner, "dp", axis=0, tiled=True)
    scores_f, is_pos, col_ok = tile_scores(
        src_emb, all_targets, 0, my_align, col_live_global, per_slot, data_size, inv_root
    )
    row_max, row_sum = row_update(start_max, scores_f, col_ok)
    col_max, col_sum = column_stats(scores_f, row_live)
    pos_score = jnp.sum(jnp.where(is_pos, scores_f, 0.0), axis=1)
    merged_max, merged_sum = combined_all((col_max, col_sum), "dp", merge_columns)
    col_lse_all = merged_max + jnp.log(merged_sum + (1.0 - col_live_gathered))
    col_lse_global = jnp.zeros((pair_rows,), jnp.float32).at[gathered_index].set(col_lse_all)
    row_lse = row_max + jnp.log(row_sum + (1.0 - row_live.astype(jnp.float32)))
    terms = jnp.where(row_live, row_lse + col_lse_global[my_align] - 2.0 * pos_score, 0.0)
    loss_total = lax.psum(jnp.sum(terms), "dp")
    pair_loss = (loss_total / live_count.astype(jnp.float32)).reshape(1)
    grad_tile = grad_block(scores_f, is_pos, col_ok, row_lse, col_lse_all, row_live, weight)
    grad_rows = jnp.dot(grad_tile, all_targets, preferred_element_type=jnp.float32)
    own_terms = lax.psum_scatter(
        lax.dot_general(
            grad_tile, src_emb, (((0,), (0,)), ((), ())), preferred_element_type=jnp.float32
        ),
        "dp",
        scatter_dimension=0,
        tiled=True,
    )
    grad_src = (grad_rows * inv_root).astype(jnp.bfloat16)
    grad_local = (own_terms * inv_root).astype(jnp.bfloat16)
    returned = lax.all_to_all(
        grad_local.reshape(1, row_count, emb_width), "lang", split_axis=1, concat_axis=0, tiled=True
    )
    grad_tgt = returned[slot_group]
    return (grad_src, grad_tgt, pair_loss)


def solution(mesh):
    in_specs = (
        P(("lang", "dp"), None),
        P(None, ("lang", "dp"), None),
        P(),
        P(),
        P("lang", None),
        P(),
    )
    out_specs = (P(("lang", "dp"), None), P(None, ("lang", "dp"), None), P("lang"))
    return jax.shard_map(
        per_device, mesh=mesh, in_specs=in_specs, out_specs=out_specs, check_vma=False
    )
```

profile of v0, /device:TPU:2, one launch (start us, length us, event | category | flops | bytes accessed | tf_op | source)
XLA Modules:
  0.0 611.2 jit_solution(6739788015881884098)
XLA Ops:
  8.6 1.5 gather_fusion.1
  10.0 10.7 %all_to_all.21 = bf16[8,16,768]{2,1,0:T(8,128)(2,1)} all-to-all(bf16[8,16,768]{2,1,0:T(8,128)(2,1)S(1)} %gather_fusion.1), channel_id=1, replica_groups=mesh['lang'=8,'dp'=32] {'lang'}, dimensions={0} | all-to-all | bytes 393216 | tf_op jit(solution)/shard_map/all_to_all | solution.py:85
  20.8 1.2 dynamic_slice.32
  22.1 1.3 dynamic_slice.31
  24.8 15.5 %scatter_custom_fusion = f32[4096]{0:T(1024)S(1)} fusion(s32[4096]{0:T(1024)S(1)} %bitcast.43, f32[4096]{0:T(1024)S(1)} %fusion.29, f32[]{:T(128)} %constant.134.clone.1), kind=kCustom, calls=%fused_computation.80 | custom fusion | bytes 16388 | tf_op jit(solution)/shard_map/scatter | solution.py:94
  40.4 23.0 %gather_fusion = f32[4096]{0:T(1024)S(1)} fusion(f32[4096]{0:T(1024)S(1)} %scatter_custom_fusion, s32[4096]{0:T(1024)S(1)} %broadcast_clamp_fusion), kind=kCustom, calls=%fused_computation | custom fusion | bytes 49152 | tf_op jit(solution)/shard_map/gather | solution.py:38
  65.5 45.6 %all-gather.4.cloned.1.call-done = bf16[4096,768]{1,0:T(8,128)(2,1)} async-done(((bf16[128,768]{1,0:T(8,128)(2,1)}), bf16[4096,768]{1,0:T(8,128)(2,1)}) %all-gather.4.cloned.1.call-update) | async-done | bytes 6291472 | tf_op jit(solution)/shard_map/all_gather | solution.py:102
  111.1 4.9 select_reduce_fusion.3
  116.0 48.0 %all-gather = f32[131072]{0:T(1024)S(1)} all-gather(f32[4096]{0:T(1024)S(1)} %get-tuple-element.142), channel_id=2, replica_groups=mesh['lang'=8,'dp'=32] {'dp'}, dimensions={0}, use_global_device_ids=true | all-gather | bytes 540672 | tf_op jit(solution)/shard_map/all_gather | solution.py:12
  164.2 4.1 fusion.6
  168.3 47.5 %all-gather.1 = f32[131072]{0:T(1024)S(1)} all-gather(f32[4096]{0:T(1024)S(1)} %get-tuple-element.139), channel_id=3, replica_groups=mesh['lang'=8,'dp'=32] {'dp'}, dimensions={0}, use_global_device_ids=true | all-gather | bytes 540672 | tf_op jit(solution)/shard_map/all_gather | solution.py:12
  216.6 30.5 %while.17 = (s32[]{:T(128)}, f32[4096]{0:T(1024)S(1)}, f32[4096]{0:T(1024)S(1)}, f32[32,4096]{1,0:T(8,128)S(1)}, f32[32,4096]{1,0:T(8,128)}, /*index=5*/s32[]{:T(128)}, s32[]{:T(128)}, s32[]{:T(128)}) while((s32[]{:T(128)}, f32[4096]{0:T(1024)S(1)}, f32[4096]{0:T(1024)S(1)}, f32[32,4096]{1,0:T(8,128)S(1)}, f32[32,4096]{1,0:T(8,128)}, ...), condition=%wide.region_7.8_spmd, body=%wide.region_6.7_spmd.sunk | while | flops 24581 | bytes 163971 | solution.py:18
  220.5 0.9 constant_dynamic-slice_fusion.4
  221.5 0.9 constant_dynamic-slice_fusion.4
  222.5 0.9 constant_dynamic-slice_fusion.4
  223.5 0.9 constant_dynamic-slice_fusion.4
  224.5 0.9 constant_dynamic-slice_fusion.4
  229.4 0.9 constant_dynamic-slice_fusion.4
  230.4 0.9 constant_dynamic-slice_fusion.4
  231.3 0.9 constant_dynamic-slice_fusion.4
  232.3 0.9 constant_dynamic-slice_fusion.4
  247.1 15.5 %scatter_custom_fusion.2 = f32[4096]{0:T(1024)S(1)} fusion(s32[4096]{0:T(1024)S(1)} %bitcast.42, f32[4096]{0:T(1024)S(1)} %log_add_fusion, f32[]{:T(128)} %constant.134.clone.1), kind=kCustom, calls=%fused_computation.78 | custom fusion | bytes 16388 | tf_op jit(solution)/shard_map/scatter | solution.py:111
  262.6 1.1 gather_fusion.3
  263.8 1.3 select_reduce_fusion.4
  265.1 9.0 %fusion.39 = f32[4096,768]{1,0:T(8,128)} fusion(bf16[128,768]{1,0:T(8,128)(2,1)S(1)} %copy-done, f32[128,4096]{0,1:T(8,128)S(1)} %get-tuple-element.159, f32[4096]{0:T(1024)S(1)} %log_add_fusion, f32[128]{0:T(128)S(1)} %get-tuple-element.156, s32[128]{0:T(128)S(1)} %fusion.38, f32[]{:T(128)} %bitcast.2, s32[4096]{0:T(1024)S(1)} %fusion.19, ...), kind=kOutput, calls=%fused_computation.97 | convolution fusion | flops 811597824 | bytes 14914692 | tf_op jit(solution)/shard_map/dot_general | solution.py:119
  274.8 234.3 %reduce-scatter.2.cloned.1.call-done = f32[128,768]{1,0:T(8,128)} async-done(((f32[4096,768]{1,0:T(8,128)}), f32[128,768]{1,0:T(8,128)}) %reduce-scatter.2.cloned.1.call-update) | async-done | bytes 393232 | tf_op jit(solution)/shard_map/reduce_scatter | solution.py:118
  509.1 1.0 fusion.8
  510.9 1.8 reduce
  513.5 5.0 all-to-all-start.1
  518.4 10.0 %fusion.7 = bf16[128,768]{1,0:T(8,128)(2,1)} fusion(bf16[4096,768]{1,0:T(8,128)(2,1)} %all-gather.4.cloned.1.call-done, f32[128,4096]{0,1:T(8,128)S(1)} %get-tuple-element.159, f32[4096]{0:T(1024)S(1)} %log_add_fusion, f32[128]{0:T(128)S(1)} %get-tuple-element.156, s32[128]{0:T(128)S(1)} %fusion.38, f32[]{:T(128)} %bitcast.2, s32[4096]{0:T(1024)S(1)} %fusion.19, ...), kind=kOutput, calls=%fused_computation.28 | convolution fusion | flops 811794432 | bytes 8623236 | tf_op jit(solution)/shard_map/dot_general | solution.py:117
  528.4 72.7 %psum.7 = f32[]{:T(128)} all-reduce(f32[]{:T(128)} %get-tuple-element.155), channel_id=1, replica_groups=mesh['lang'=8,'dp'=32] {'dp'}, use_global_device_ids=true, to_apply=%region_12.13 | all-reduce | flops 1 | bytes 8 | tf_op jit(solution)/shard_map/psum | solution.py:114
  602.0 1.2 gather_fusion.2
  (87 shorter events, 28.9 us)
Async XLA Ops:
  7.2 103.9 %copy-start = (bf16[128,768]{1,0:T(8,128)(2,1)S(1)}, bf16[128,768]{1,0:T(8,128)(2,1)}, u32[]{:S(2)}) copy-start(bf16[128,768]{1,0:T(8,128)(2,1)} %param.8) | copy-start | bytes 589828
  7.2 103.9 %all-gather.4.cloned.1.call-start = ((), (), s32[]{:S(2)}) async-start(), calls=%async_computation.3 | async-start | bytes 6488064 | tf_op jit(solution)/shard_map/all_gather | solution.py:102
  20.8 488.3 %reduce-scatter.2.cloned.1.call-start = ((), (), s32[]{:S(2)}) async-start(), calls=%async_computation.4 | async-start | bytes 12976128 | tf_op jit(solution)/shard_map/reduce_scatter | solution.py:118
  513.5 88.3 %all-to-all-start.1 = ((bf16[8,2,6144]{2,1,0:T(2,128)(2,1)}), bf16[8,2,6144]{2,1,0:T(2,128)(2,1)S(1)}, u32[]{:S(2)}, u32[]{:S(2)}) async-start(bf16[8,2,6144]{2,1,0:T(2,128)(2,1)} %reshape.359), calls=%async_computation.2 | async-start | bytes 393216 | tf_op jit(solution)/shard_map/all_to_all | solution.py:128
Sparse Core Ops, SparseCore 0:
  20.9 90.1 all-gather.3
  274.2 234.7 reduce-scatter.1
where the time goes:
time: 612 us; the launch traced here: 611 us
  waiting for transfers between devices  280 us (46%)
  blocking collectives  179 us (29%)
  local copies, waits for them, and re-layouts  93.5 us (15%)
  matrix products  23.9 us (4%)
  between operations  16.7 us (3%)
  other arithmetic  12.5 us (2%)
    reduce_scatter x1, waiting for transfers between devices, per_device(): lax.psum_scatter(lax.dot_general(grad_tile, src_emb, (((0,), (0,)), ((),...  234 us
    all_gather x2, blocking collectives, combined_all(): everything = jax.tree.map(lambda part: lax.all_gather(part, axis), value)  95.5 us
    psum x1, blocking collectives, per_device(): loss_total = lax.psum(jnp.sum(terms), 'dp')  72.7 us
    all_gather x1, waiting for transfers between devices, per_device(): all_targets = lax.all_gather(partner, 'dp', axis=0, tiled=True)  45.6 us
    dynamic_slice x31, local copies, waits for them, and re-layouts, lap(): return combine(so_far, jax.tree.map(lambda part: part[k], everything))  29 us
    gather x1, local copies, waits for them, and re-layouts, tile_scores(): col_ok = col_live_global[tgt_index] > 0.5  23 us
    scatter x1, local copies, waits for them, and re-layouts, per_device(): jnp.zeros((pair_rows,), jnp.float32).at[gathered_index].set(col_lse_all)  15.5 us
    scatter x1, local copies, waits for them, and re-layouts, per_device(): col_live_global = jnp.zeros((pair_rows,), jnp.float32).at[pair_align].set...  15.5 us
  transfers between devices with their start and end apart: 3, of which 2 were waited for; matrix products, arithmetic and copies ran while one was open for 9% of the time, Pallas kernels for 0%

commit v1 on v0

--- a/solution.py
+++ b/solution.py
@@ -6,6 +6,15 @@
 
 MARGIN = 0.3
 LOW_FILL = -1e30
+spans_create = lambda x_local, array_dim: jnp.concatenate(
+    lax.all_to_all(
+        jnp.stack([x_local for _ in range(lax.psum(1, axis_name="dp"))]),
+        "dp",
+        split_axis=0,
+        concat_axis=0,
+    ),
+    axis=array_dim,
+)
 
 
 def combined_all(value, axis, combine):
@@ -99,7 +108,7 @@
     gathered_index = target_index(0, pair_rows, row_count, per_slot, data_size)
     col_live_gathered = col_live_global[gathered_index]
     start_max = jnp.full((row_count,), LOW_FILL, jnp.float32)
-    all_targets = lax.all_gather(partner, "dp", axis=0, tiled=True)
+    all_targets = spans_create(partner, 0)
     scores_f, is_pos, col_ok = tile_scores(
         src_emb, all_targets, 0, my_align, col_live_global, per_slot, data_size, inv_root
     )

time: 612 us -> 682 us (1.11)
  waiting for transfers between devices: 280 us -> 332 us
  starting transfers between devices: 5.06 us -> 16.5 us
    all_to_all x0 -> x1, waiting for transfers between devices: none -> 96.6 us  [lax.all_to_all(jnp.stack([x_local for _ in range(lax.psum(1, axis_name='d...]
    all_gather x1 -> x0, waiting for transfers between devices: 45.6 us -> none  [per_device(): all_targets = lax.all_gather(partner, 'dp', axis=0, tiled=True)]
    all_to_all x0 -> x1, starting transfers between devices: none -> 11.7 us  [lax.all_to_all(jnp.stack([x_local for _ in range(lax.psum(1, axis_name='d...]
  transfers between devices with their start and end apart: 3 -> 3, of which waited for: 2 -> 2; matrix products, arithmetic and copies ran while one was open for 9% -> 8% of each run, Pallas kernels for 0% -> 0%
where the time goes in v1:
time: 682 us; the launch traced here: 680 us
  waiting for transfers between devices  332 us (49%)
  blocking collectives  185 us (27%)
  local copies, waits for them, and re-layouts  94.9 us (14%)
  matrix products  23.9 us (4%)
  between operations  16.7 us (2%)
  starting transfers between devices  16.5 us (2%)
  other arithmetic  11.1 us (2%)
    reduce_scatter x1, waiting for transfers between devices, per_device(): lax.psum_scatter(lax.dot_general(grad_tile, src_emb, (((0,), (0,)), ((),...  235 us
    all_gather x2, blocking collectives, combined_all(): everything = jax.tree.map(lambda part: lax.all_gather(part, axis), value)  102 us
    all_to_all x1, waiting for transfers between devices, lax.all_to_all(jnp.stack([x_local for _ in range(lax.psum(1, axis_name='d...  96.6 us
    psum x1, blocking collectives, per_device(): loss_total = lax.psum(jnp.sum(terms), 'dp')  72.7 us
    dynamic_slice x31, local copies, waits for them, and re-layouts, lap(): return combine(so_far, jax.tree.map(lambda part: part[k], everything))  29 us
    gather x1, local copies, waits for them, and re-layouts, tile_scores(): col_ok = col_live_global[tgt_index] > 0.5  23 us
    scatter x1, local copies, waits for them, and re-layouts, per_device(): jnp.zeros((pair_rows,), jnp.float32).at[gathered_index].set(col_lse_all)  15.5 us
    scatter x1, local copies, waits for them, and re-layouts, per_device(): col_live_global = jnp.zeros((pair_rows,), jnp.float32).at[pair_align].set...  15.5 us
  transfers between devices with their start and end apart: 3, of which 2 were waited for; matrix products, arithmetic and copies ran while one was open for 8% of the time, Pallas kernels for 0%

profile of v1, /device:TPU:2, one launch (start us, length us, event | category | flops | bytes accessed | tf_op | source)
XLA Modules:
  0.0 680.3 jit_solution(5210258846228634929)
XLA Ops:
  8.5 1.5 gather_fusion.1
  10.0 10.0 %all_to_all.29 = bf16[8,16,768]{2,1,0:T(8,128)(2,1)S(1)} all-to-all(bf16[8,16,768]{2,1,0:T(8,128)(2,1)S(1)} %gather_fusion.1), channel_id=1, replica_groups=mesh['lang'=8,'dp'=32] {'lang'}, dimensions={0} | all-to-all | bytes 393216 | tf_op jit(solution)/shard_map/all_to_all | solution.py:94
  20.1 3.4 stack.3
  23.4 11.7 %all-to-all-start.1 = ((bf16[32,128,768]{2,1,0:T(8,128)(2,1)}), bf16[32,128,768]{2,1,0:T(8,128)(2,1)}, u32[]{:S(2)}, u32[]{:S(2)}) async-start(bf16[32,128,768]{2,1,0:T(8,128)(2,1)} %stack.3), calls=%async_computation.1 | async-start | bytes 12582912 | tf_op jit(solution)/shard_map/all_to_all | solution.py:10
  37.1 15.5 %scatter_custom_fusion = f32[4096]{0:T(1024)S(1)} fusion(s32[4096]{0:T(1024)S(1)} %bitcast.44, f32[4096]{0:T(1024)S(1)} %fusion.29, f32[]{:T(128)} %constant.134.clone.1), kind=kCustom, calls=%fused_computation.80 | custom fusion | bytes 16388 | tf_op jit(solution)/shard_map/scatter | solution.py:103
  52.8 23.0 %gather_fusion = f32[4096]{0:T(1024)S(1)} fusion(f32[4096]{0:T(1024)S(1)} %scatter_custom_fusion, s32[4096]{0:T(1024)S(1)} %broadcast_clamp_fusion), kind=kCustom, calls=%fused_computation | custom fusion | bytes 49152 | tf_op jit(solution)/shard_map/gather | solution.py:47
  76.6 96.6 %all-to-all-done.1 = bf16[32,128,768]{2,1,0:T(8,128)(2,1)} async-done(((bf16[32,128,768]{2,1,0:T(8,128)(2,1)}), bf16[32,128,768]{2,1,0:T(8,128)(2,1)}, u32[]{:S(2)}, u32[]{:S(2)}) %all-to-all-start.1) | async-done | bytes 6291488 | tf_op jit(solution)/shard_map/all_to_all | solution.py:10
  173.1 4.9 select_reduce_fusion.3
  178.1 53.1 %all-gather = f32[131072]{0:T(1024)S(1)} all-gather(f32[4096]{0:T(1024)S(1)} %get-tuple-element.142), channel_id=2, replica_groups=mesh['lang'=8,'dp'=32] {'dp'}, dimensions={0}, use_global_device_ids=true | all-gather | bytes 540672 | tf_op jit(solution)/shard_map/all_gather | solution.py:21
  231.3 4.1 fusion.6
  235.4 48.8 %all-gather.1 = f32[131072]{0:T(1024)S(1)} all-gather(f32[4096]{0:T(1024)S(1)} %get-tuple-element.139), channel_id=3, replica_groups=mesh['lang'=8,'dp'=32] {'dp'}, dimensions={0}, use_global_device_ids=true | all-gather | bytes 540672 | tf_op jit(solution)/shard_map/all_gather | solution.py:21
  285.1 30.4 %while.17 = (s32[]{:T(128)}, f32[4096]{0:T(1024)S(1)}, f32[4096]{0:T(1024)S(1)}, f32[32,4096]{1,0:T(8,128)S(1)}, f32[32,4096]{1,0:T(8,128)}, /*index=5*/s32[]{:T(128)}, s32[]{:T(128)}, s32[]{:T(128)}) while((s32[]{:T(128)}, f32[4096]{0:T(1024)S(1)}, f32[4096]{0:T(1024)S(1)}, f32[32,4096]{1,0:T(8,128)S(1)}, f32[32,4096]{1,0:T(8,128)}, ...), condition=%wide.region_7.8_spmd, body=%wide.region_6.7_spmd.sunk | while | flops 24581 | bytes 163971 | solution.py:27
  286.0 0.9 constant_dynamic-slice_fusion.4
  288.0 0.9 constant_dynamic-slice_fusion.4
  290.0 0.9 constant_dynamic-slice_fusion.4
  292.9 0.9 constant_dynamic-slice_fusion.4
  294.9 0.9 constant_dynamic-slice_fusion.4
  296.8 0.9 constant_dynamic-slice_fusion.4
  297.8 0.9 constant_dynamic-slice_fusion.4
  299.8 0.9 constant_dynamic-slice_fusion.4
  301.8 0.9 constant_dynamic-slice_fusion.4
  315.5 15.5 %scatter_custom_fusion.2 = f32[4096]{0:T(1024)S(1)} fusion(s32[4096]{0:T(1024)S(1)} %bitcast.43, f32[4096]{0:T(1024)S(1)} %log_add_fusion, f32[]{:T(128)} %constant.134.clone.1), kind=kCustom, calls=%fused_computation.78 | custom fusion | bytes 16388 | tf_op jit(solution)/shard_map/scatter | solution.py:120
  331.1 1.1 gather_fusion.3
  332.2 1.3 select_reduce_fusion.4
  333.5 9.0 %fusion.39 = f32[4096,768]{1,0:T(8,128)} fusion(bf16[128,768]{1,0:T(8,128)(2,1)S(1)} %copy-done, f32[128,4096]{0,1:T(8,128)S(1)} %get-tuple-element.159, f32[4096]{0:T(1024)S(1)} %log_add_fusion, f32[128]{0:T(128)S(1)} %get-tuple-element.156, s32[128]{0:T(128)S(1)} %fusion.38, f32[]{:T(128)} %bitcast.2, s32[4096]{0:T(1024)S(1)} %fusion.19, ...), kind=kOutput, calls=%fused_computation.97 | convolution fusion | flops 811597824 | bytes 14914692 | tf_op jit(solution)/shard_map/dot_general | solution.py:128
  343.2 235.2 %reduce-scatter.2.cloned.1.call-done = f32[128,768]{1,0:T(8,128)} async-done(((f32[4096,768]{1,0:T(8,128)}), f32[128,768]{1,0:T(8,128)}) %reduce-scatter.2.cloned.1.call-update) | async-done | bytes 393232 | tf_op jit(solution)/shard_map/reduce_scatter | solution.py:127
  578.4 1.0 fusion.8
  580.2 1.8 reduce
  582.8 4.8 all-to-all-start.2
  587.6 10.0 %fusion.7 = bf16[128,768]{1,0:T(8,128)(2,1)} fusion(bf16[4096,768]{1,0:T(8,128)(2,1)} %bitcast.8, f32[128,4096]{0,1:T(8,128)S(1)} %get-tuple-element.159, f32[4096]{0:T(1024)S(1)} %log_add_fusion, f32[128]{0:T(128)S(1)} %get-tuple-element.156, s32[128]{0:T(128)S(1)} %fusion.38, f32[]{:T(128)} %bitcast.2, s32[4096]{0:T(1024)S(1)} %fusion.19, ...), kind=kOutput, calls=%fused_computation.28 | convolution fusion | flops 811794432 | bytes 8623236 | tf_op jit(solution)/shard_map/dot_general | solution.py:126
  597.5 72.7 %psum.7 = f32[]{:T(128)} all-reduce(f32[]{:T(128)} %get-tuple-element.155), channel_id=1, replica_groups=mesh['lang'=8,'dp'=32] {'dp'}, use_global_device_ids=true, to_apply=%region_12.13 | all-reduce | flops 1 | bytes 8 | tf_op jit(solution)/shard_map/psum | solution.py:123
  671.1 1.2 gather_fusion.2
  (93 shorter events, 28.1 us)
Async XLA Ops:
  7.2 166.0 %copy-start = (bf16[128,768]{1,0:T(8,128)(2,1)S(1)}, bf16[128,768]{1,0:T(8,128)(2,1)}, u32[]{:S(2)}) copy-start(bf16[128,768]{1,0:T(8,128)(2,1)} %param.8) | copy-start | bytes 589828
  23.4 11.8 %copy-start.2 = (s32[8]{0:T(128)S(1)}, s32[8]{0:T(128)}, u32[]{:S(2)}) copy-start(s32[8]{0:T(128)} %param.11) | copy-start | bytes 100
  23.4 12.4 %copy-start.3 = (f32[8]{0:T(128)S(1)}, f32[8]{0:T(128)}, u32[]{:S(2)}) copy-start(f32[8]{0:T(128)} %param.13) | copy-start | bytes 100
  23.4 13.7 %copy-start.1 = (s32[1,4096]{1,0:T(1,128)S(1)}, s32[1,4096]{1,0:T(1,128)}, u32[]{:S(2)}) copy-start(s32[1,4096]{1,0:T(1,128)} %param.12) | copy-start | bytes 49156
  23.4 149.7 %all-to-all-start.1 = ((bf16[32,128,768]{2,1,0:T(8,128)(2,1)}), bf16[32,128,768]{2,1,0:T(8,128)(2,1)}, u32[]{:S(2)}, u32[]{:S(2)}) async-start(bf16[32,128,768]{2,1,0:T(8,128)(2,1)} %stack.3), calls=%async_computation.1 | async-start | bytes 12582912 | tf_op jit(solution)/shard_map/all_to_all | solution.py:10
  35.1 543.3 %reduce-scatter.2.cloned.1.call-start = ((), (), s32[]{:S(2)}) async-start(), calls=%async_computation.4 | async-start | bytes 12976128 | tf_op jit(solution)/shard_map/reduce_scatter | solution.py:127
  582.8 88.1 %all-to-all-start.2 = ((bf16[8,2,6144]{2,1,0:T(2,128)(2,1)}), bf16[8,2,6144]{2,1,0:T(2,128)(2,1)S(1)}, u32[]{:S(2)}, u32[]{:S(2)}) async-start(bf16[8,2,6144]{2,1,0:T(2,128)(2,1)} %reshape.364), calls=%async_computation.3 | async-start | bytes 393216 | tf_op jit(solution)/shard_map/all_to_all | solution.py:137
Sparse Core Ops, SparseCore 0:
  342.7 235.6 reduce-scatter.1
